TPU v7x, 256 devices: a whole 4x4x8 slice. The times are simulated.
256 devices in a mesh: chan: 64 (over z, y, core), row: 4 (over x).
Axes of the slice: x: 4, y: 4, z: 8, core: 2. Of those that a mesh axis runs over, the one named last changes fastest.
Arguments:
- generator: float32 [64, 1280, 1280], P('chan', 'row'), as said below
- hamiltonian: float32 [64, 1280, 1280], P('chan', 'row'), as said below
- recoupling: float32 [64, 1280, 1280], P('chan')
- channel_size: int32 [64], P('chan'), may hold values from 128 to 1280, as said below
- hole_first: int32 [64, 1280], P('chan'), may hold values 0 or 1
- hole_second: int32 [64, 1280], P('chan'), may hold values 0 or 1
Outputs:
- derivative: float32 [64, 1280, 1280], P('chan', 'row')
Inputs may be any that keep to these rules, and one draw needn't show every extreme that they name: generator is antisymmetric and hamiltonian symmetric in every channel block. hamiltonian is symmetric in every channel block. `channel_size`: some channel has exactly 1280 states.
All inputs are finite; a program needn't handle non-finite values. No bound on the sum of `hole_first` or of `hole_second` on one device may be relied on, other than what follows from the above.
Results may differ from a plain program's by a relative error of at most 0.000076.
Values sent between devices are 32-bit elements; how exact they have to be, the bound alone decides.
No kernel may reach another device: no remote copies, remote signals or barrier semaphores. Data moves between devices by JAX's collectives and lax.ppermute only.
A program may use at most 128 MiB of HBM per device.

v0:
```python
import jax
import jax.numpy as jnp
from jax import lax
from jax.sharding import PartitionSpec as P


def batched(left, right):
    return jnp.einsum("cij,cjk->cik", left, right, precision=lax.Precision.HIGHEST)


def shards(generator, hamiltonian, recoupling, channel_size, hole_first, hole_second):
    local_count = generator.shape[0]
    row_count = generator.shape[1]
    block_order = generator.shape[2]
    chan_count = lax.axis_size("chan")
    row_index = lax.axis_index("row")
    positions = jnp.arange(block_order, dtype=jnp.int32)
    inside = (positions[None, :] < channel_size[:, None]).astype(jnp.float32)
    row_inside = lax.dynamic_slice_in_dim(inside, row_index * row_count, row_count, 1)
    block_mask = row_inside[:, :, None] * inside[:, None, :]
    gen_live = generator * block_mask
    ham_live = hamiltonian * block_mask
    weight_pp = (1 - hole_first - hole_second).astype(jnp.float32)
    weight_ph = (hole_first - hole_second).astype(jnp.float32)
    piece_shape = (local_count, row_count, chan_count, block_order // chan_count)
    gen_moved, ham_moved = (
        lax.all_to_all(
            gen_live.reshape(piece_shape), "chan", split_axis=2, concat_axis=2, tiled=True
        ),
        lax.all_to_all(
            ham_live.reshape(piece_shape), "chan", split_axis=2, concat_axis=2, tiled=True
        ),
    )
    gen_bar = batched(gen_moved.reshape(generator.shape), recoupling)
    ham_bar = batched(ham_moved.reshape(generator.shape), recoupling)
    pieces = (
        lax.all_gather(gen_bar, "row", axis=1, tiled=True),
        lax.all_gather(ham_bar, "row", axis=1, tiled=True),
    )
    factor = weight_ph[:, None, :]
    gen_cols = gen_bar * factor
    ham_cols = ham_bar * factor
    ph_term = batched(gen_cols, pieces[1]) - batched(ham_cols, pieces[0])
    turned = jnp.einsum("cij,ckj->cik", ph_term, recoupling, precision=lax.Precision.HIGHEST)
    back_moved = lax.all_to_all(
        turned.reshape(piece_shape), "chan", split_axis=2, concat_axis=2, tiled=True
    )
    ph_back = back_moved.reshape(generator.shape)
    pieces = (
        lax.all_gather(gen_live, "row", axis=1, tiled=True),
        lax.all_gather(ham_live, "row", axis=1, tiled=True),
    )
    factor = weight_pp[:, None, :]
    gen_cols = gen_live * factor
    ham_cols = ham_live * factor
    ladder = batched(gen_cols, pieces[1]) - batched(ham_cols, pieces[0])
    return (ladder + ph_back) * block_mask


def solution(mesh):
    in_specs = (
        P("chan", "row", None),
        P("chan", "row", None),
        P("chan", None, None),
        P("chan"),
        P("chan", None),
        P("chan", None),
    )
    out_specs = P("chan", "row", None)
    return jax.shard_map(shards, mesh=mesh, in_specs=in_specs, out_specs=out_specs, check_vma=False)
```

profile of v0, /device:TPU:1, one launch (start us, length us, event | category | flops | bytes accessed | tf_op | source)
XLA Modules:
  0.0 404.9 jit_solution(18243573594442668754)
XLA Ops:
  6.5 0.0 all-gather.11.cloned.1.call-start
  7.2 2.2 multiply_multiply_fusion.1
  9.4 0.0 copy-start.1
  9.5 0.0 copy-start.5
  9.5 3.6 copy.20
  13.0 0.0 copy-done.1
  13.0 60.2 %all_to_all.15 = f32[1,320,64,20]{1,0,3,2:T(1,128)} all-to-all(f32[1,320,64,20]{1,0,3,2:T(1,128)} %bitcast.47), channel_id=1, replica_groups=mesh['chan'=64,'row'=4] {'chan'}, dimensions={2} | all-to-all | bytes 3276800 | tf_op jit(solution)/shard_map/all_to_all | solution.py:30
  73.2 7.7 %reduce.4 = f32[320,64,20]{0,2,1:T(8,128)} reduce(f32[1,320,64,20]{1,0,3,2:T(1,128)} %all_to_all.15, f32[]{:T(128)} %constant.18), dimensions={0}, to_apply=%all_to_all.10.reduce_sub_computation | reduce | bytes 3276804 | tf_op jit(solution)/shard_map/all_to_all | solution.py:30
  81.0 2.9 reshape.159
  83.8 11.5 %fusion = f32[320,1280]{1,0:T(8,128)} fusion(f32[320,1280]{0,1:T(8,128)} %reshape.159, f32[1,1280,1280]{2,1,0:T(8,128)} %param.8), kind=kOutput, calls=%fused_computation | convolution fusion | flops 6291456000 | bytes 9830400 | tf_op jit(solution)/shard_map/cij,cjk->cik/dot_general | solution.py:8
  95.3 0.0 all-gather.11.cloned.1.call-update
  95.3 0.0 all-gather.13.cloned.1.call-start
  95.4 0.0 copy-done.5
  95.4 3.2 copy.19
  98.6 54.1 %all_to_all.16 = f32[1,320,64,20]{1,0,3,2:T(1,128)S(1)} all-to-all(f32[1,320,64,20]{1,0,3,2:T(1,128)} %bitcast.48), channel_id=1, replica_groups=mesh['chan'=64,'row'=4] {'chan'}, dimensions={2} | all-to-all | bytes 3276800 | tf_op jit(solution)/shard_map/all_to_all | solution.py:27
  152.6 7.0 %reduce.2 = f32[320,64,20]{0,2,1:T(8,128)} reduce(f32[1,320,64,20]{1,0,3,2:T(1,128)S(1)} %all_to_all.16, f32[]{:T(128)} %constant.18), dimensions={0}, to_apply=%all_to_all.9.reduce_sub_computation | reduce | bytes 3276804 | tf_op jit(solution)/shard_map/all_to_all | solution.py:27
  159.6 2.0 reshape.156
  161.6 10.9 %fusion.2 = f32[320,1280]{1,0:T(8,128)} fusion(f32[320,1280]{0,1:T(8,128)S(1)} %reshape.156, f32[1,1280,1280]{2,1,0:T(8,128)} %param.8), kind=kOutput, calls=%fused_computation.2 | convolution fusion | flops 6291456000 | bytes 9830400 | tf_op jit(solution)/shard_map/cij,cjk->cik/dot_general | solution.py:8
  172.5 0.0 all-gather.13.cloned.1.call-update
  172.5 0.0 all-gather.9.cloned.1.call-start
  172.5 0.7 all-gather.9.cloned.1.call-update
  173.2 0.0 all-gather.7.cloned.1.call-start
  173.3 0.5 all-gather.7.cloned.1.call-update
  173.8 0.0 copy-start.7
  173.8 0.0 copy-start.8
  173.8 0.0 copy-start.4
  173.8 8.4 %dot_general.37 = f32[64,20,1280]{2,1,0:T(8,128)} reshape(f32[1,1280,1280]{2,1,0:T(8,128)} %param.8) | data formatting | bytes 13107200 | tf_op jit(solution)/shard_map/cij,ckj->cik/dot_general | solution.py:44
  182.3 0.0 copy-done.7
  182.3 0.0 copy-done.8
  182.3 0.0 all-gather.11.cloned.1.call-done
  182.4 0.0 copy-done.4
  182.4 0.0 copy-start.3
  182.4 11.7 %fusion.26 = f32[320,1280]{1,0:T(8,128)} fusion(f32[1280,1280]{1,0:T(8,128)} %all-gather.11.cloned.1.call-done, f32[320,1280]{1,0:T(8,128)S(1)} %copy-done.4, f32[1280]{0:T(1024)S(1)} %get-tuple-element.6), kind=kOutput, calls=%fused_computation.21 | convolution fusion | flops 6291865600 | bytes 9835520 | tf_op jit(solution)/shard_map/cij,cjk->cik/dot_general | solution.py:8
  194.0 46.6 %all-gather.13.cloned.1.call-done = f32[1280,1280]{1,0:T(8,128)} async-done(((f32[320,1280]{1,0:T(8,128)}), f32[1280,1280]{1,0:T(8,128)}) %all-gather.13.cloned.1.call-update) | async-done | bytes 6553616 | tf_op jit(solution)/shard_map/all_gather | solution.py:37
  240.6 0.0 copy-done.3
  240.6 10.5 %fusion.19 = f32[320,1280,1]{1,0,2:T(8,128)S(1)} fusion(f32[320,1280]{1,0:T(8,128)} %fusion.26, f32[1280,1280]{1,0:T(8,128)} %all-gather.13.cloned.1.call-done, f32[320,1280]{1,0:T(8,128)S(1)} %copy-done.3, f32[1280]{0:T(1024)S(1)} %get-tuple-element.6), kind=kOutput, calls=%fused_computation.14 | convolution fusion | flops 6292275200 | bytes 11473920 | tf_op jit(solution)/shard_map/cij,cjk->cik/dot_general | solution.py:8
  251.2 0.0 copy-done
  251.2 11.5 %fusion.30 = f32[1,320,64,20]{1,2,3,0:T(8,128)S(1)} fusion(f32[320,1280,1]{1,0,2:T(8,128)S(1)} %fusion.19, f32[64,20,1280]{2,1,0:T(8,128)S(1)} %copy-done), kind=kOutput, calls=%fused_computation.25 | convolution fusion | flops 6291456000 | bytes 9830400 | tf_op jit(solution)/shard_map/cij,ckj->cik/dot_general | solution.py:44
  262.7 3.3 copy.22
  266.0 11.0 %all-to-all-start.2 = ((f32[1,320,64,20]{1,0,3,2:T(1,128)}), f32[1,320,64,20]{1,0,3,2:T(1,128)}, u32[]{:S(2)}, u32[]{:S(2)}) async-start(f32[1,320,64,20]{1,0,3,2:T(1,128)} %copy.22), calls=%async_computation.2 | async-start | bytes 3932160 | tf_op jit(solution)/shard_map/all_to_all | solution.py:45
  277.0 36.6 %all-gather.9.cloned.1.call-done = f32[1,1280,1280]{2,1,0:T(8,128)} async-done(((f32[1,320,1280]{2,1,0:T(8,128)}), f32[1,1280,1280]{2,1,0:T(8,128)}) %all-gather.9.cloned.1.call-update) | async-done | bytes 6553616 | tf_op jit(solution)/shard_map/all_gather | solution.py:50
  313.6 10.9 %fusion.4 = f32[320,1280]{1,0:T(8,128)} fusion(f32[1,1280,1280]{2,1,0:T(8,128)} %all-gather.9.cloned.1.call-done, f32[1,320,1280]{2,1,0:T(8,128)S(1)} %copy-done.2, f32[1280]{0:T(1024)S(1)} %get-tuple-element.5), kind=kOutput, calls=%fused_computation.4 | convolution fusion | flops 6291865600 | bytes 9835520 | tf_op jit(solution)/shard_map/cij,cjk->cik/dot_general | solution.py:8
  324.5 0.0 all-to-all-done.2
  324.5 6.3 %reduce.5 = f32[320,64,20]{0,2,1:T(8,128)S(1)} reduce(f32[1,320,64,20]{1,0,3,2:T(1,128)} %all-to-all-done.2, f32[]{:T(128)} %constant.18), dimensions={0}, to_apply=%all_to_all.11.reduce_sub_computation | reduce | bytes 3276804 | tf_op jit(solution)/shard_map/all_to_all | solution.py:45
  330.8 1.5 reshape.162
  332.3 2.3 copy.23
  334.6 51.8 %all-gather.7.cloned.1.call-done = f32[1,1280,1280]{2,1,0:T(8,128)} async-done(((f32[1,320,1280]{2,1,0:T(8,128)}), f32[1,1280,1280]{2,1,0:T(8,128)}) %all-gather.7.cloned.1.call-update) | async-done | bytes 6553616 | tf_op jit(solution)/shard_map/all_gather | solution.py:51
  386.4 11.5 %fusion.20 = f32[1,320,1280]{2,1,0:T(8,128)} fusion(f32[320,1280]{1,0:T(8,128)S(1)} %copy.23, f32[320,1280]{1,0:T(8,128)} %fusion.4, f32[1,1280,1280]{2,1,0:T(8,128)} %all-gather.7.cloned.1.call-done, f32[1280]{0:T(1024)S(1)} %fusion.37, f32[320]{0:T(512)S(1)} %fusion.38, f32[1280]{0:T(1024)S(1)} %get-tuple-element.5, f32[1,320,1280]{2,1,0:T(8,128)S(1)} %copy-done.6), kind=kOutput, calls=%fused_computation.15 | convolution fusion | flops 6294323200 | bytes 13118720 | tf_op jit(solution)/shard_map/cij,cjk->cik/dot_general | solution.py:8
  (8 shorter events, 0.1 us)
Async XLA Ops:
  6.5 175.8 %all-gather.11.cloned.1.call-start = ((), (), s32[]{:S(2)}) async-start(), calls=%async_computation.5 | async-start | bytes 8192000 | tf_op jit(solution)/shard_map/all_gather | solution.py:38
  9.4 3.6 copy-start.1
  9.5 85.9 %copy-start.5 = (f32[1,320,1280]{2,1,0:T(8,128)}, f32[1,320,1280]{2,1,0:T(8,128)S(1)}, u32[]{:S(2)}) copy-start(f32[1,320,1280]{2,1,0:T(8,128)S(1)} %get-tuple-element.7) | copy-start | bytes 4915204
  95.3 145.3 %all-gather.13.cloned.1.call-start = ((), (), s32[]{:S(2)}) async-start(), calls=%async_computation.6 | async-start | bytes 8192000 | tf_op jit(solution)/shard_map/all_gather | solution.py:37
  172.5 141.1 %all-gather.9.cloned.1.call-start = ((), (), s32[]{:S(2)}) async-start(), calls=%async_computation.4 | async-start | bytes 8192000 | tf_op jit(solution)/shard_map/all_gather | solution.py:50
  173.2 213.2 %all-gather.7.cloned.1.call-start = ((), (), s32[]{:S(2)}) async-start(), calls=%async_computation.3 | async-start | bytes 8192000 | tf_op jit(solution)/shard_map/all_gather | solution.py:51
  173.8 8.5 %copy-start.7 = (s32[1,1280]{1,0:T(1,128)S(1)}, s32[1,1280]{1,0:T(1,128)}, u32[]{:S(2)}) copy-start(s32[1,1280]{1,0:T(1,128)} %param.11) | copy-start | bytes 15364
  173.8 8.5 %copy-start.8 = (s32[1,1280]{1,0:T(1,128)S(1)}, s32[1,1280]{1,0:T(1,128)}, u32[]{:S(2)}) copy-start(s32[1,1280]{1,0:T(1,128)} %param.10) | copy-start | bytes 15364
  173.8 8.5 %copy-start.4 = (f32[320,1280]{1,0:T(8,128)S(1)}, f32[320,1280]{1,0:T(8,128)}, u32[]{:S(2)}) copy-start(f32[320,1280]{1,0:T(8,128)} %fusion.2) | copy-start | bytes 4915204
  182.4 58.2 %copy-start.3 = (f32[320,1280]{1,0:T(8,128)S(1)}, f32[320,1280]{1,0:T(8,128)}, u32[]{:S(2)}) copy-start(f32[320,1280]{1,0:T(8,128)} %fusion) | copy-start | bytes 4915204
  240.6 10.5 %copy-start = (f32[64,20,1280]{2,1,0:T(8,128)S(1)}, f32[64,20,1280]{2,1,0:T(8,128)}, u32[]{:S(2)}) copy-start(f32[64,20,1280]{2,1,0:T(8,128)} %dot_general.37) | copy-start | bytes 19660804
  266.0 47.6 %copy-start.2 = (f32[1,320,1280]{2,1,0:T(8,128)S(1)}, f32[1,320,1280]{2,1,0:T(8,128)}, u32[]{:S(2)}) copy-start(f32[1,320,1280]{2,1,0:T(8,128)} %copy-done.1) | copy-start | bytes 4915204
  266.0 58.5 %all-to-all-start.2 = ((f32[1,320,64,20]{1,0,3,2:T(1,128)}), f32[1,320,64,20]{1,0,3,2:T(1,128)}, u32[]{:S(2)}, u32[]{:S(2)}) async-start(f32[1,320,64,20]{1,0,3,2:T(1,128)} %copy.22), calls=%async_computation.2 | async-start | bytes 3932160 | tf_op jit(solution)/shard_map/all_to_all | solution.py:45
  332.3 54.2 %copy-start.6 = (f32[1,320,1280]{2,1,0:T(8,128)S(1)}, f32[1,320,1280]{2,1,0:T(8,128)}, u32[]{:S(2)}) copy-start(f32[1,320,1280]{2,1,0:T(8,128)} %param.6) | copy-start | bytes 4915204
Sparse Core Ops, SparseCore 0:
  95.4 67.9 all-gather.10
  172.6 67.9 all-gather.12
  242.4 71.1 all-gather.8
  315.3 71.1 all-gather.6
where the time goes:
time: 411 us; the launch traced here: 405 us
  waiting for transfers between devices  136 us (33%)
  blocking collectives  114 us (28%)
  matrix products  78.5 us (19%)
  local copies, waits for them, and re-layouts  27.1 us (7%)
  other arithmetic  23.3 us (6%)
  between operations  14.4 us (4%)
  starting transfers between devices  11.2 us (3%)
    dot_general x6, matrix products, batched(): jnp.einsum('cij,cjk->cik', left, right, precision=lax.Precision.HIGHEST)  66.9 us
    all_to_all x1, blocking collectives, shards(): lax.all_to_all(ham_live.reshape(piece_shape), 'chan', split_axis=2, conca...  60.2 us
    all_to_all x1, blocking collectives, shards(): lax.all_to_all(gen_live.reshape(piece_shape), 'chan', split_axis=2, conca...  54.1 us
    all_gather x1, waiting for transfers between devices, shards(): lax.all_gather(ham_live, 'row', axis=1, tiled=True)  51.8 us
    all_gather x1, waiting for transfers between devices, shards(): lax.all_gather(gen_bar, 'row', axis=1, tiled=True)  46.6 us
    all_gather x1, waiting for transfers between devices, shards(): lax.all_gather(gen_live, 'row', axis=1, tiled=True)  36.6 us
    dot_general x2, local copies, waits for them, and re-layouts, shards(): jnp.einsum('cij,ckj->cik', ph_term, recoupling, precision=lax.Precision.H...  11.7 us
    dot_general x1, matrix products, shards(): jnp.einsum('cij,ckj->cik', ph_term, recoupling, precision=lax.Precision.H...  11.5 us
  transfers between devices with their start and end apart: 5, of which 3 were waited for; matrix products, arithmetic and copies ran while one was open for 22% of the time, Pallas kernels for 0%

commit v1 on v0

--- a/solution.py
+++ b/solution.py
@@ -2,6 +2,12 @@
 import jax.numpy as jnp
 from jax import lax
 from jax.sharding import PartitionSpec as P
+
+
+def carry_ratios(work_x, mesh_name, d0):
+    current_arr = jnp.stack([work_x for _ in range(jax.lax.axis_size(mesh_name))])
+    p_next = jax.lax.all_to_all(current_arr, mesh_name, 0, 0)
+    return jnp.concatenate(p_next, axis=d0)
 
 
 def batched(left, right):
@@ -46,10 +52,7 @@
         turned.reshape(piece_shape), "chan", split_axis=2, concat_axis=2, tiled=True
     )
     ph_back = back_moved.reshape(generator.shape)
-    pieces = (
-        lax.all_gather(gen_live, "row", axis=1, tiled=True),
-        lax.all_gather(ham_live, "row", axis=1, tiled=True),
-    )
+    pieces = (carry_ratios(gen_live, "row", 1), lax.all_gather(ham_live, "row", axis=1, tiled=True))
     factor = weight_pp[:, None, :]
     gen_cols = gen_live * factor
     ham_cols = ham_live * factor

time: 411 us -> 426 us (1.036)
  the two profiles are of different devices: /device:TPU:1 before, /device:TPU:4 now
where the time goes in v1:
time: 426 us; the launch traced here: 420 us
  waiting for transfers between devices  141 us (33%)
  blocking collectives  115 us (27%)
  matrix products  78.8 us (18%)
  local copies, waits for them, and re-layouts  32.3 us (8%)
  other arithmetic  25.5 us (6%)
  between operations  14.4 us (3%)
  starting transfers between devices  12.8 us (3%)
    all_gather x1, waiting for transfers between devices, shards(): lax.all_gather(gen_bar, 'row', axis=1, tiled=True)  103 us
    dot_general x6, matrix products, batched(): jnp.einsum('cij,cjk->cik', left, right, precision=lax.Precision.HIGHEST)  67.3 us
    all_to_all x1, blocking collectives, shards(): lax.all_to_all(ham_live.reshape(piece_shape), 'chan', split_axis=2, conca...  60.8 us
    all_to_all x1, blocking collectives, shards(): lax.all_to_all(gen_live.reshape(piece_shape), 'chan', split_axis=2, conca...  54.2 us
    all_to_all x1, waiting for transfers between devices, shards(): lax.all_to_all(turned.reshape(piece_shape), 'chan', split_axis=2, concat_...  37.5 us
    dot_general x2, local copies, waits for them, and re-layouts, shards(): jnp.einsum('cij,ckj->cik', ph_term, recoupling, precision=lax.Precision.H...  11.8 us
    dot_general x1, matrix products, shards(): jnp.einsum('cij,ckj->cik', ph_term, recoupling, precision=lax.Precision.H...  11.5 us
  transfers between devices with their start and end apart: 5, of which 2 were waited for; matrix products, arithmetic and copies ran while one was open for 23% of the time, Pallas kernels for 0%

profile of v1, /device:TPU:4, one launch (start us, length us, event | category | flops | bytes accessed | tf_op | source)
XLA Modules:
  0.0 420.0 jit_solution(7049729380476262008)
XLA Ops:
  6.5 0.0 all-gather.8.cloned.1.call-start
  7.2 2.2 multiply_multiply_fusion.1
  9.4 0.0 copy-start.1
  9.5 3.4 copy.20
  12.9 0.0 copy-done.1
  12.9 60.8 %all_to_all.20 = f32[1,320,64,20]{1,0,3,2:T(1,128)} all-to-all(f32[1,320,64,20]{1,0,3,2:T(1,128)} %bitcast.48), channel_id=1, replica_groups=mesh['chan'=64,'row'=4] {'chan'}, dimensions={2} | all-to-all | bytes 3276800 | tf_op jit(solution)/shard_map/all_to_all | solution.py:36
  73.7 7.7 %reduce.4 = f32[320,64,20]{0,2,1:T(8,128)} reduce(f32[1,320,64,20]{1,0,3,2:T(1,128)} %all_to_all.20, f32[]{:T(128)} %constant.18), dimensions={0}, to_apply=%all_to_all.14.reduce_sub_computation | reduce | bytes 3276804 | tf_op jit(solution)/shard_map/all_to_all | solution.py:36
  81.4 2.9 reshape.164
  84.3 11.5 %fusion = f32[320,1280]{1,0:T(8,128)} fusion(f32[320,1280]{0,1:T(8,128)} %reshape.164, f32[1,1280,1280]{2,1,0:T(8,128)} %param.8), kind=kOutput, calls=%fused_computation | convolution fusion | flops 6291456000 | bytes 9830400 | tf_op jit(solution)/shard_map/cij,cjk->cik/dot_general | solution.py:14
  95.8 0.0 all-gather.8.cloned.1.call-update
  95.8 0.0 all-gather.10.cloned.1.call-start
  95.8 3.2 copy.19
  99.1 54.2 %all_to_all.21 = f32[1,320,64,20]{1,0,3,2:T(1,128)} all-to-all(f32[1,320,64,20]{1,0,3,2:T(1,128)} %bitcast.49), channel_id=1, replica_groups=mesh['chan'=64,'row'=4] {'chan'}, dimensions={2} | all-to-all | bytes 3276800 | tf_op jit(solution)/shard_map/all_to_all | solution.py:33
  153.3 7.7 %reduce.2 = f32[320,64,20]{0,2,1:T(8,128)} reduce(f32[1,320,64,20]{1,0,3,2:T(1,128)} %all_to_all.21, f32[]{:T(128)} %constant.18), dimensions={0}, to_apply=%all_to_all.13.reduce_sub_computation | reduce | bytes 3276804 | tf_op jit(solution)/shard_map/all_to_all | solution.py:33
  161.0 2.9 reshape.161
  164.0 11.5 %fusion.2 = f32[320,1280]{1,0:T(8,128)} fusion(f32[320,1280]{0,1:T(8,128)} %reshape.161, f32[1,1280,1280]{2,1,0:T(8,128)} %param.8), kind=kOutput, calls=%fused_computation.2 | convolution fusion | flops 6291456000 | bytes 9830400 | tf_op jit(solution)/shard_map/cij,cjk->cik/dot_general | solution.py:14
  175.5 0.0 all-gather.10.cloned.1.call-update
  175.5 0.0 all-gather.6.cloned.1.call-start
  175.5 0.7 all-gather.6.cloned.1.call-update
  176.2 3.2 stack.2
  179.4 5.8 %all-to-all-start = ((f32[4,1,320,1280]{3,2,1,0:T(8,128)}), f32[4,1,320,1280]{3,2,1,0:T(8,128)}, u32[]{:S(2)}, u32[]{:S(2)}) async-start(f32[4,1,320,1280]{3,2,1,0:T(8,128)} %stack.2), calls=%async_computation | async-start | bytes 13107200 | tf_op jit(solution)/shard_map/all_to_all | solution.py:9
  185.2 0.0 copy-start.4
  185.2 0.0 copy-start.5
  185.2 8.5 %dot_general.37 = f32[64,20,1280]{2,1,0:T(8,128)} reshape(f32[1,1280,1280]{2,1,0:T(8,128)} %param.8) | data formatting | bytes 13107200 | tf_op jit(solution)/shard_map/cij,ckj->cik/dot_general | solution.py:50
  193.7 0.0 copy-done.4
  193.7 0.0 copy-done.5
  193.8 0.0 all-gather.8.cloned.1.call-done
  193.8 0.0 copy-start.3
  193.8 11.5 %fusion.25 = f32[320,1280]{1,0:T(8,128)} fusion(f32[1280,1280]{1,0:T(8,128)} %all-gather.8.cloned.1.call-done, f32[320,1280]{1,0:T(8,128)} %fusion.2, f32[1280]{0:T(1024)S(1)} %get-tuple-element.6), kind=kOutput, calls=%fused_computation.20 | convolution fusion | flops 6291865600 | bytes 9835520 | tf_op jit(solution)/shard_map/cij,cjk->cik/dot_general | solution.py:14
  205.3 102.9 %all-gather.10.cloned.1.call-done = f32[1280,1280]{1,0:T(8,128)} async-done(((f32[320,1280]{1,0:T(8,128)}), f32[1280,1280]{1,0:T(8,128)}) %all-gather.10.cloned.1.call-update) | async-done | bytes 6553616 | tf_op jit(solution)/shard_map/all_gather | solution.py:43
  308.2 0.0 copy-done.3
  308.2 0.0 copy-start
  308.2 10.5 %fusion.17 = f32[320,1280,1]{1,0,2:T(8,128)S(1)} fusion(f32[320,1280]{1,0:T(8,128)} %fusion.25, f32[1280,1280]{1,0:T(8,128)} %all-gather.10.cloned.1.call-done, f32[320,1280]{1,0:T(8,128)S(1)} %copy-done.3, f32[1280]{0:T(1024)S(1)} %get-tuple-element.6), kind=kOutput, calls=%fused_computation.12 | convolution fusion | flops 6292275200 | bytes 11473920 | tf_op jit(solution)/shard_map/cij,cjk->cik/dot_general | solution.py:14
  318.7 0.0 copy-done
  318.8 11.5 %fusion.29 = f32[1,320,64,20]{1,2,3,0:T(8,128)S(1)} fusion(f32[320,1280,1]{1,0,2:T(8,128)S(1)} %fusion.17, f32[64,20,1280]{2,1,0:T(8,128)S(1)} %copy-done), kind=kOutput, calls=%fused_computation.24 | convolution fusion | flops 6291456000 | bytes 9830400 | tf_op jit(solution)/shard_map/cij,ckj->cik/dot_general | solution.py:50
  330.3 3.3 copy.22
  333.6 0.0 copy-start.2
  333.6 0.0 all-to-all-done
  333.6 7.0 %all-to-all-start.3 = ((f32[1,320,64,20]{1,0,3,2:T(1,128)}), f32[1,320,64,20]{1,0,3,2:T(1,128)}, u32[]{:S(2)}, u32[]{:S(2)}) async-start(f32[1,320,64,20]{1,0,3,2:T(1,128)} %copy.22), calls=%async_computation.3 | async-start | bytes 3932160 | tf_op jit(solution)/shard_map/all_to_all | solution.py:51
  340.6 0.0 copy-done.2
  340.6 10.9 %fusion.21 = f32[320,1280]{1,0:T(8,128)} fusion(f32[1280,1280]{1,0:T(8,128)} %bitcast.5, f32[1,320,1280]{2,1,0:T(8,128)S(1)} %copy-done.2, f32[1280]{0:T(1024)S(1)} %get-tuple-element.5), kind=kOutput, calls=%fused_computation.16 | convolution fusion | flops 6291865600 | bytes 9835520 | tf_op jit(solution)/shard_map/cij,cjk->cik/dot_general | solution.py:14
  351.5 37.5 %all-to-all-done.3 = f32[1,320,64,20]{1,0,3,2:T(1,128)} async-done(((f32[1,320,64,20]{1,0,3,2:T(1,128)}), f32[1,320,64,20]{1,0,3,2:T(1,128)}, u32[]{:S(2)}, u32[]{:S(2)}) %all-to-all-start.3) | async-done | bytes 1638432 | tf_op jit(solution)/shard_map/all_to_all | solution.py:51
  389.0 7.7 %reduce.5 = f32[320,64,20]{0,2,1:T(8,128)} reduce(f32[1,320,64,20]{1,0,3,2:T(1,128)} %all-to-all-done.3, f32[]{:T(128)} %constant.18), dimensions={0}, to_apply=%all_to_all.15.reduce_sub_computation | reduce | bytes 3276804 | tf_op jit(solution)/shard_map/all_to_all | solution.py:51
  396.8 2.7 reshape.167
  399.5 2.1 copy.23
  401.6 0.0 all-gather.6.cloned.1.call-done
  401.6 11.4 %fusion.18 = f32[1,320,1280]{2,1,0:T(8,128)} fusion(f32[320,1280]{1,0:T(8,128)S(1)} %copy.23, f32[320,1280]{1,0:T(8,128)} %fusion.21, f32[1,1280,1280]{2,1,0:T(8,128)} %all-gather.6.cloned.1.call-done, f32[1,320,1280]{2,1,0:T(8,128)S(1)} %get-tuple-element.7, f32[1280]{0:T(1024)S(1)} %fusion.36, f32[320]{0:T(512)S(1)} %fusion.37, f32[1280]{0:T(1024)S(1)} %get-tuple-element.5), kind=kOutput, calls=%fused_computation.13 | convolution fusion | flops 6293504000 | bytes 13118720 | tf_op jit(solution)/shard_map/cij,cjk->cik/dot_general | solution.py:14
  (3 shorter events, 0.1 us)
Async XLA Ops:
  6.5 187.3 %all-gather.8.cloned.1.call-start = ((), (), s32[]{:S(2)}) async-start(), calls=%async_computation.5 | async-start | bytes 8192000 | tf_op jit(solution)/shard_map/all_gather | solution.py:44
  9.4 3.5 copy-start.1
  95.8 212.4 %all-gather.10.cloned.1.call-start = ((), (), s32[]{:S(2)}) async-start(), calls=%async_computation.6 | async-start | bytes 8192000 | tf_op jit(solution)/shard_map/all_gather | solution.py:43
  175.5 226.1 %all-gather.6.cloned.1.call-start = ((), (), s32[]{:S(2)}) async-start(), calls=%async_computation.4 | async-start | bytes 8192000 | tf_op jit(solution)/shard_map/all_gather | solution.py:55
  179.4 154.2 %all-to-all-start = ((f32[4,1,320,1280]{3,2,1,0:T(8,128)}), f32[4,1,320,1280]{3,2,1,0:T(8,128)}, u32[]{:S(2)}, u32[]{:S(2)}) async-start(f32[4,1,320,1280]{3,2,1,0:T(8,128)} %stack.2), calls=%async_computation | async-start | bytes 13107200 | tf_op jit(solution)/shard_map/all_to_all | solution.py:9
  185.2 8.5 %copy-start.4 = (s32[1,1280]{1,0:T(1,128)S(1)}, s32[1,1280]{1,0:T(1,128)}, u32[]{:S(2)}) copy-start(s32[1,1280]{1,0:T(1,128)} %param.11) | copy-start | bytes 15364
  185.2 8.5 %copy-start.5 = (s32[1,1280]{1,0:T(1,128)S(1)}, s32[1,1280]{1,0:T(1,128)}, u32[]{:S(2)}) copy-start(s32[1,1280]{1,0:T(1,128)} %param.10) | copy-start | bytes 15364
  193.8 114.4 %copy-start.3 = (f32[320,1280]{1,0:T(8,128)S(1)}, f32[320,1280]{1,0:T(8,128)}, u32[]{:S(2)}) copy-start(f32[320,1280]{1,0:T(8,128)} %fusion) | copy-start | bytes 4915204
  308.2 10.5 %copy-start = (f32[64,20,1280]{2,1,0:T(8,128)S(1)}, f32[64,20,1280]{2,1,0:T(8,128)}, u32[]{:S(2)}) copy-start(f32[64,20,1280]{2,1,0:T(8,128)} %dot_general.37) | copy-start | bytes 19660804
  333.6 7.0 %copy-start.2 = (f32[1,320,1280]{2,1,0:T(8,128)S(1)}, f32[1,320,1280]{2,1,0:T(8,128)}, u32[]{:S(2)}) copy-start(f32[1,320,1280]{2,1,0:T(8,128)} %copy-done.1) | copy-start | bytes 4915204
  333.6 55.4 %all-to-all-start.3 = ((f32[1,320,64,20]{1,0,3,2:T(1,128)}), f32[1,320,64,20]{1,0,3,2:T(1,128)}, u32[]{:S(2)}, u32[]{:S(2)}) async-start(f32[1,320,64,20]{1,0,3,2:T(1,128)} %copy.22), calls=%async_computation.3 | async-start | bytes 3932160 | tf_op jit(solution)/shard_map/all_to_all | solution.py:51
Sparse Core Ops, SparseCore 0:
  95.9 65.9 all-gather.7
  175.6 132.5 all-gather.9
  310.0 67.2 all-gather.5
